TPU v7x, 32 devices: a whole 2x2x4 slice. The times are simulated.
32 devices in a mesh: dp: 4 (over z), fsdp: 8 (over y, x, core).
Axes of the slice: x: 2, y: 2, z: 4, core: 2. Of those that a mesh axis runs over, the one named last changes fastest.
Arguments:
- item_hidden: bfloat16 [2048, 2048], P(('dp', 'fsdp')), may hold values from -400 to 400
- item_gain: float32 [2048], replicated, may hold values from 0.25 to 1.75
- history: int32 [4096], P(('dp', 'fsdp')), may hold values from 0 to 255, as said below
- owner_map: int32 [8, 256], P('fsdp'), may hold values from 0 to 255, as said below
- user_gain: float32 [2048], replicated, may hold values from 0.25 to 1.75
- value_weight: bfloat16 [2048, 2048], P('fsdp'), may hold values from -0.125 to 0.125
- value_grad: bfloat16 [4096, 2048], P(('dp', 'fsdp')), may hold values from -6 to 6
Outputs:
- values: bfloat16 [4096, 2048], P(('dp', 'fsdp'))
- item_grad: float32 [2048, 2048], P(('dp', 'fsdp'))
Inputs may be any that keep to these rules, and one draw needn't show every extreme that they name: `history`: storage row s of catalog c is row s % 64 of the items on dp index s // 64 and fsdp index c. In each aligned block of 128 positions, the positions name at most 8 distinct items stored on any one dp index, and exactly 8 for some dp index. `owner_map`: each row is a permutation.
All inputs are finite; a program needn't handle non-finite values.
Results may differ from a plain program's by a relative error of at most 0.0057.
Values may be sent and summed in bfloat16 or wider, within the bound.
A program may use at most 64 MiB of HBM per device.

v0:
```python
import jax
import jax.numpy as jnp
from jax import lax
from jax.sharding import PartitionSpec as P

CAP = 8


eps = 1e-06


def norm_rows(values, gain):
    scale = lax.rsqrt(jnp.mean(values * values, axis=1, keepdims=True) + eps)
    return (values * scale * gain, scale)


def norm_back(values, gain, scale, upstream):
    unit = values * scale
    scaled = upstream * gain
    return scale * (scaled - unit * jnp.mean(scaled * unit, axis=1, keepdims=True))


def locate(owner_row, items):
    matches = items[:, None] == lax.broadcasted_iota(
        jnp.int32, (items.shape[0], owner_row.shape[0]), 1
    )
    return jnp.sum(jnp.where(matches, owner_row[None, :], 0), axis=1)


def local(item_hidden, item_gain, history, owner_map, user_gain, value_weight, value_grad):
    groups = lax.axis_size("dp")
    here = lax.axis_index("dp")
    item_rows = item_hidden.shape[0]
    hist_rows = history.shape[0]
    width = item_hidden.shape[1]
    owner_row = owner_map[0]
    pool = owner_row.shape[0]
    hidden = item_hidden.astype(jnp.float32)
    item_emb, item_scale = norm_rows(hidden, item_gain)
    item_emb = item_emb.astype(jnp.bfloat16)
    all_history = lax.all_gather(history, "dp", axis=0, tiled=True)
    stored_all = locate(owner_row, all_history).reshape(groups, hist_rows)
    local_rows = lax.broadcasted_iota(jnp.int32, (groups, hist_rows, item_rows), 2)
    wanted = jnp.any(stored_all[:, :, None] == here * item_rows + local_rows, axis=1)
    slot = jnp.cumsum(wanted.astype(jnp.int32), axis=1) - 1
    slot_ids = lax.broadcasted_iota(jnp.int32, (groups, CAP, item_rows), 1)
    select = (wanted[:, None, :] & (slot[:, None, :] == slot_ids)).astype(jnp.bfloat16)
    outgoing = jnp.einsum(
        "dcr,rk->dck", select, item_emb, preferred_element_type=jnp.float32
    ).astype(jnp.bfloat16)
    incoming = lax.all_to_all(outgoing, "dp", split_axis=0, concat_axis=0, tiled=True)
    stored = locate(owner_row, history)
    pick = stored[:, None] == lax.broadcasted_iota(jnp.int32, (hist_rows, pool), 1)
    own_wanted = jnp.any(pick, axis=0).reshape(groups, item_rows)
    own_slot = (jnp.cumsum(own_wanted.astype(jnp.int32), axis=1) - 1).reshape(pool)
    slot_pos = jnp.sum(jnp.where(pick, own_slot[None, :], 0), axis=1)
    buffer_row = stored // item_rows * CAP + slot_pos
    x = jnp.take(incoming.reshape(groups * CAP, width), buffer_row, axis=0).astype(jnp.float32)
    normed, scale = norm_rows(x, user_gain)
    normed = normed.astype(jnp.bfloat16)
    whole = lax.all_gather(value_weight, "fsdp", axis=0, tiled=True)
    values = jnp.dot(normed, whole, preferred_element_type=jnp.float32)
    upstream = lax.dot_general(
        value_grad, whole, (((1,), (1,)), ((), ())), preferred_element_type=jnp.float32
    )
    values = values.astype(jnp.bfloat16)
    dx = norm_back(x, user_gain, scale, upstream)
    one_hot = (
        buffer_row[:, None] == lax.broadcasted_iota(jnp.int32, (hist_rows, groups * CAP), 1)
    ).astype(jnp.float32)
    summed = lax.dot_general(
        one_hot,
        dx,
        (((0,), (0,)), ((), ())),
        precision=lax.Precision.HIGHEST,
        preferred_element_type=jnp.float32,
    )
    returned = lax.all_to_all(
        summed.astype(jnp.bfloat16).reshape(groups, CAP, width),
        "dp",
        split_axis=0,
        concat_axis=0,
        tiled=True,
    )
    emb_grad = jnp.einsum("dcr,dck->rk", select, returned, preferred_element_type=jnp.float32)
    item_grad = norm_back(hidden, item_gain, item_scale, emb_grad)
    return (values, item_grad)


def solution(mesh):
    in_specs = (
        P(("dp", "fsdp"), None),
        P(),
        P(("dp", "fsdp")),
        P("fsdp", None),
        P(),
        P("fsdp", None),
        P(("dp", "fsdp"), None),
    )
    out_specs = (P(("dp", "fsdp"), None), P(("dp", "fsdp"), None))
    return jax.shard_map(local, mesh=mesh, in_specs=in_specs, out_specs=out_specs, check_vma=False)
```

profile of v0, /device:TPU:0, one launch (start us, length us, event | category | flops | bytes accessed | tf_op | source)
XLA Modules:
  0.0 94.1 jit_solution(9549017904262749175)
XLA Ops:
  7.2 0.0 copy-start
  7.2 0.0 all-gather.3.cloned.1.call-start
  7.2 0.7 all-gather.3.cloned.1.call-update
  7.9 12.7 %all-gather = s32[4,1,128]{2,1,0:T(1,128)S(1)} all-gather(s32[1,1,128]{2,1,0:T(1,128)} %bitcast.39), channel_id=1, replica_groups=mesh['dp'=4,'fsdp'=8] {'dp'}, dimensions={0}, use_global_device_ids=true | all-gather | bytes 2560 | tf_op jit(solution)/shard_map/all_gather | solution.py:41
  20.6 0.9 select_reduce_fusion
  21.6 0.2 compare_reduce_fusion
  21.8 0.2 reduce_window_sum.18
  22.0 1.1 %fusion.18 = f32[64]{0:T(128)S(1)} fusion(bf16[64,2048]{1,0:T(8,128)(2,1)} %param.7), kind=kLoop, calls=%fused_computation.27 | loop fusion | flops 393152 | bytes 262400 | tf_op jit(solution)/shard_map/reduce_sum | solution.py:13
  23.2 1.9 %convolution_convert_fusion.2 = bf16[4,8,2048]{2,1,0:T(8,128)(2,1)} fusion(bf16[64,2048]{1,0:T(8,128)(2,1)} %param.7, f32[2048]{0:T(1024)} %param.8, f32[64]{0:T(128)S(1)} %add_rsqrt_fusion.1, s32[4,64]{1,0:T(4,128)S(1)} %broadcast_add_fusion, pred[4,64]{1,0:T(4,128)(4,1)S(1)} %compare_reduce_fusion), kind=kOutput, calls=%fused_computation.6 | convolution fusion | flops 8982528 | bytes 402944 | tf_op jit(solution)/shard_map/dcr,rk->dck/dot_general | solution.py:48
  25.0 3.3 %all-to-all-start = ((bf16[4,8,2048]{2,1,0:T(8,128)(2,1)}), bf16[4,8,2048]{2,1,0:T(8,128)(2,1)S(1)}, u32[]{:S(2)}, u32[]{:S(2)}) async-start(bf16[4,8,2048]{2,1,0:T(8,128)(2,1)} %convolution_convert_fusion.2), calls=%async_computation | async-start | bytes 262144 | tf_op jit(solution)/shard_map/all_to_all | solution.py:51
  28.4 0.9 select_reduce_fusion.2
  29.2 0.1 fusion.28
  29.3 0.1 reshape.140
  29.4 0.2 reduce_window_sum.17
  29.7 0.1 sub.24
  29.8 0.2 select_reduce_fusion.1
  30.0 4.2 %all-to-all-done = bf16[4,8,2048]{2,1,0:T(8,128)(2,1)S(1)} async-done(((bf16[4,8,2048]{2,1,0:T(8,128)(2,1)}), bf16[4,8,2048]{2,1,0:T(8,128)(2,1)S(1)}, u32[]{:S(2)}, u32[]{:S(2)}) %all-to-all-start) | async-done | bytes 131104 | tf_op jit(solution)/shard_map/all_to_all | solution.py:51
  34.2 0.0 copy-start.2
  34.2 0.9 gather_fusion
  35.2 0.3 fusion.10
  35.5 31.5 %all-gather.3.cloned.1.call-done = bf16[2048,2048]{1,0:T(8,128)(2,1)} async-done(((bf16[256,2048]{1,0:T(8,128)(2,1)}), bf16[2048,2048]{1,0:T(8,128)(2,1)}) %all-gather.3.cloned.1.call-update) | async-done | bytes 8388624 | tf_op jit(solution)/shard_map/all_gather | solution.py:61
  67.0 0.0 copy-done
  67.0 6.4 %fusion.6 = (f32[128]{0:T(128)S(1)}, f32[128,2048]{1,0:T(8,128)S(1)}) fusion(f32[128]{0:T(128)S(1)} %add_rsqrt_fusion, bf16[128,2048]{1,0:T(8,128)(2,1)S(1)} %gather_fusion, pred[128]{0:T(512)(128)(4,1)S(1)} %get-tuple-element.2, f32[2048]{0:T(1024)} %param.11, bf16[128,2048]{1,0:T(8,128)(2,1)S(1)} %copy-done, ...), kind=kOutput, calls=%fused_computation.14 | convolution fusion | flops 1075314560 | bytes 10495104 | tf_op jit(solution)/shard_map/dot_general | solution.py:63
  73.4 1.4 %fusion.1 = bf16[4,8,2048]{2,1,0:T(8,128)(2,1)} fusion(f32[128,2048]{1,0:T(8,128)S(1)} %get-tuple-element.5, f32[128]{0:T(128)S(1)} %broadcast_multiply_fusion, f32[128]{0:T(128)S(1)} %add_rsqrt_fusion, s32[128]{0:T(128)S(1)} %get-tuple-element.3, bf16[128,2048]{1,0:T(8,128)(2,1)S(1)} %gather_fusion, pred[128]{0:T(512)(128)(4,1)S(1)} %get-tuple-element.2), kind=kOutput, calls=%fused_computation.7 | convolution fusion | flops 102305792 | bytes 1705600 | tf_op jit(solution)/shard_map/dot_general | solution.py:71
  74.8 4.7 %all-to-all-start.1 = ((bf16[4,8,2048]{2,1,0:T(8,128)(2,1)}), bf16[4,8,2048]{2,1,0:T(8,128)(2,1)S(1)}, u32[]{:S(2)}, u32[]{:S(2)}) async-start(bf16[4,8,2048]{2,1,0:T(8,128)(2,1)} %fusion.1), calls=%async_computation.1 | async-start | bytes 262144 | tf_op jit(solution)/shard_map/all_to_all | solution.py:78
  79.6 0.0 copy-done.2
  79.6 5.5 %convolution_convert_fusion = bf16[128,2048]{1,0:T(8,128)(2,1)} fusion(bf16[2048,2048]{1,0:T(8,128)(2,1)} %all-gather.3.cloned.1.call-done, f32[2048]{0:T(1024)S(1)} %copy-done.2, f32[128]{0:T(128)S(1)} %add_rsqrt_fusion, bf16[128,2048]{1,0:T(8,128)(2,1)S(1)} %gather_fusion, pred[128]{0:T(512)(128)(4,1)S(1)} %get-tuple-element.2), kind=kOutput, calls=%fused_computation.2 | convolution fusion | flops 1075314688 | bytes 9446016 | tf_op jit(solution)/shard_map/dot_general | solution.py:62
  85.0 0.9 all-to-all-done.1
  85.9 0.0 copy-done.1
  85.9 0.0 copy-done.3
  85.9 0.4 fusion.15
  86.3 1.0 %fusion.17 = f32[64,2048]{1,0:T(8,128)} fusion(f32[64,2048]{1,0:T(8,128)S(1)} %get-tuple-element.7, bf16[64,2048]{1,0:T(8,128)(2,1)S(1)} %copy-done.1, f32[64]{0:T(128)S(1)} %broadcast_multiply_fusion.1, f32[64]{0:T(128)S(1)} %add_rsqrt_fusion.1), kind=kLoop, calls=%fused_computation.26 | loop fusion | flops 655360 | bytes 1311232 | tf_op jit(solution)/shard_map/mul | solution.py:20
  (14 shorter events, 0.1 us)
Async XLA Ops:
  7.2 59.9 %copy-start = (bf16[128,2048]{1,0:T(8,128)(2,1)S(1)}, bf16[128,2048]{1,0:T(8,128)(2,1)}, u32[]{:S(2)}) copy-start(bf16[128,2048]{1,0:T(8,128)(2,1)} %param.13) | copy-start | bytes 1572868
  7.2 59.8 %all-gather.3.cloned.1.call-start = ((), (), s32[]{:S(2)}) async-start(), calls=%async_computation.2 | async-start | bytes 9437184 | tf_op jit(solution)/shard_map/all_gather | solution.py:61
  25.0 9.2 %all-to-all-start = ((bf16[4,8,2048]{2,1,0:T(8,128)(2,1)}), bf16[4,8,2048]{2,1,0:T(8,128)(2,1)S(1)}, u32[]{:S(2)}, u32[]{:S(2)}) async-start(bf16[4,8,2048]{2,1,0:T(8,128)(2,1)} %convolution_convert_fusion.2), calls=%async_computation | async-start | bytes 262144 | tf_op jit(solution)/shard_map/all_to_all | solution.py:51
  34.2 45.3 %copy-start.2 = (f32[2048]{0:T(1024)S(1)}, f32[2048]{0:T(1024)}, u32[]{:S(2)}) copy-start(f32[2048]{0:T(1024)} %param.11) | copy-start | bytes 24580
  74.8 11.1 %copy-start.1 = (bf16[64,2048]{1,0:T(8,128)(2,1)S(1)}, bf16[64,2048]{1,0:T(8,128)(2,1)}, u32[]{:S(2)}) copy-start(bf16[64,2048]{1,0:T(8,128)(2,1)} %param.7) | copy-start | bytes 786436
  74.8 11.1 %copy-start.3 = (f32[2048]{0:T(1024)S(1)}, f32[2048]{0:T(1024)}, u32[]{:S(2)}) copy-start(f32[2048]{0:T(1024)} %param.8) | copy-start | bytes 24580
  74.8 11.1 %all-to-all-start.1 = ((bf16[4,8,2048]{2,1,0:T(8,128)(2,1)}), bf16[4,8,2048]{2,1,0:T(8,128)(2,1)S(1)}, u32[]{:S(2)}, u32[]{:S(2)}) async-start(bf16[4,8,2048]{2,1,0:T(8,128)(2,1)} %fusion.1), calls=%async_computation.1 | async-start | bytes 262144 | tf_op jit(solution)/shard_map/all_to_all | solution.py:78
Sparse Core Ops, SparseCore 0:
  9.9 57.0 all-gather.2
where the time goes:
time: 94.6 us; the launch traced here: 94.1 us
  waiting for transfers between devices  37.3 us (39%)
  matrix products  15.5 us (16%)
  between operations  14.1 us (15%)
  blocking collectives  12.7 us (13%)
  starting transfers between devices  8.09 us (9%)
  other arithmetic  5.2 us (5%)
  local copies, waits for them, and re-layouts  1.12 us (1%)
    all_gather x1, waiting for transfers between devices, local(): whole = lax.all_gather(value_weight, 'fsdp', axis=0, tiled=True)  31.5 us
    all_gather x1, blocking collectives, local(): all_history = lax.all_gather(history, 'dp', axis=0, tiled=True)  12.7 us
    dot_general x1, matrix products, local(): lax.dot_general(value_grad, whole, (((1,), (1,)), ((), ())), preferred_el...  6.36 us
    dot_general x1, matrix products, local(): values = jnp.dot(normed, whole, preferred_element_type=jnp.float32)  5.48 us
    all_to_all x1, starting transfers between devices, local(): lax.all_to_all(summed.astype(jnp.bfloat16).reshape(groups, CAP, width), '...  4.73 us
    all_to_all x1, waiting for transfers between devices, local(): lax.all_to_all(outgoing, 'dp', split_axis=0, concat_axis=0, tiled=True)  4.25 us
    all_to_all x1, starting transfers between devices, local(): lax.all_to_all(outgoing, 'dp', split_axis=0, concat_axis=0, tiled=True)  3.33 us
  transfers between devices with their start and end apart: 3, of which 3 were waited for; matrix products, arithmetic and copies ran while one was open for 13% of the time, Pallas kernels for 0%

commit v1 on v0

--- a/solution.py
+++ b/solution.py
@@ -1,9 +1,15 @@
+import functools
 import jax
 import jax.numpy as jnp
 from jax import lax
+from jax.experimental import pallas as pl
+from jax.experimental.pallas import tpu as pltpu
 from jax.sharding import PartitionSpec as P
 
 CAP = 8
+MESH = pl.DeviceIdType.MESH
+f32 = jnp.float32
+bf16 = jnp.bfloat16
 
 
 eps = 1e-06
@@ -27,7 +33,7 @@
     return jnp.sum(jnp.where(matches, owner_row[None, :], 0), axis=1)
 
 
-def local(item_hidden, item_gain, history, owner_map, user_gain, value_weight, value_grad):
+def local_moving_weight(item_hidden, item_gain, history, owner_map, user_gain, value_weight, value_grad):
     groups = lax.axis_size("dp")
     here = lax.axis_index("dp")
     item_rows = item_hidden.shape[0]
@@ -87,6 +93,279 @@
     return (values, item_grad)
 
 
+def iota(shape, dim):
+    return lax.broadcasted_iota(jnp.int32, shape, dim)
+
+
+def dot(a, b, ca=1, cb=0):
+    return lax.dot_general(a, b, (((ca,), (cb,)), ((), ())), preferred_element_type=f32)
+
+
+def fold(rows):
+    half = rows.shape[1] // 2
+    return jnp.concatenate([rows[:, :half], rows[:, half:]], axis=0)
+
+
+def unfold(rows):
+    return jnp.concatenate([rows[:CAP], rows[CAP:]], axis=1)
+
+
+def stored_rows(hist, parts, item_rows):
+    pool = parts.shape[1]
+    named = (iota((pool, hist.shape[1]), 0) == hist).astype(f32).astype(bf16)
+    found = dot(parts, named)
+    return found[0:1] * item_rows + found[1:2]
+
+
+def slots(wants, item_rows):
+    lane = iota((item_rows, 128), 1)
+    wanted = jnp.zeros((item_rows, 128), f32)
+    for group, want in enumerate(wants):
+        wanted = jnp.where(lane // CAP == group, want, wanted)
+    before = (iota((item_rows, item_rows), 1) < iota((item_rows, item_rows), 0)).astype(f32)
+    slot = dot(before.astype(bf16), wanted.astype(bf16))
+    return jnp.where(slot == (lane % CAP).astype(f32), wanted, 0.0)
+
+
+def kernel(
+    groups, chips,
+    item_gain, history, owner, user_gain, item_hidden, weight, value_grad,
+    values_out, item_grad_out,
+    hidden_buf, grad_buf, w_buf, hist_buf, emb_out, emb_in, sum_buf, x_out, x_in,
+    part_own, part_out, part_in, up_out, up_in, back_out, back_in,
+    local_sem, w_sem, hist_send, hist_recv, emb_send, emb_recv, sum_send, sum_recv,
+    x_send, x_recv, part_send, part_recv, up_send, up_recv, back_send, back_recv,
+):
+    here = lax.axis_index("dp")
+    fsdp = lax.axis_index("fsdp")
+    chip = fsdp // 2
+    core = fsdp % 2
+    item_rows, width = item_hidden.shape
+    hist_rows = history.shape[1]
+    rows = groups * CAP
+    piece = width // chips
+    peers = [lax.rem(here + k, groups) for k in range(1, groups)]
+    mates = [lax.rem(chip + k, chips) for k in range(1, chips)]
+
+    def dp_id(peer):
+        return (peer, fsdp)
+
+    def chip_id(mate):
+        return (here, mate * 2 + core)
+
+    sibling = (here, chip * 2 + 1 - core)
+
+    loads = [
+        pltpu.make_async_copy(value_grad, grad_buf, local_sem.at[0]),
+        pltpu.make_async_copy(item_hidden, hidden_buf, local_sem.at[1]),
+        pltpu.make_async_copy(weight, w_buf.at[core], local_sem.at[2]),
+    ]
+    for load in loads:
+        load.start()
+
+    barrier = pltpu.get_barrier_semaphore()
+    for target in [dp_id(p) for p in peers] + [chip_id(m) for m in mates] + [sibling]:
+        pl.semaphore_signal(barrier, inc=1, device_id=target, device_id_type=MESH)
+    pl.semaphore_wait(barrier, groups + chips - 1)
+
+    def remote(src, dst, send, recv, target):
+        return pltpu.make_async_remote_copy(
+            src_ref=src, dst_ref=dst, send_sem=send, recv_sem=recv,
+            device_id=target, device_id_type=MESH,
+        )
+
+    sends = []
+
+    def send_dp(out_of, into, send, recv):
+        for k, peer in enumerate(peers):
+            copy = remote(out_of(peer), into.at[here], send.at[k], recv.at[here], dp_id(peer))
+            copy.start()
+            sends.append(copy)
+
+    def wait_dp(into, send, recv):
+        for k, peer in enumerate(peers):
+            remote(into.at[peer], into.at[peer], send.at[k], recv.at[peer], dp_id(peer)).wait_recv()
+
+    def send_chip(out_of, into, send, recv):
+        for k, mate in enumerate(mates):
+            copy = remote(out_of(mate), into.at[chip], send.at[k], recv.at[chip], chip_id(mate))
+            copy.start()
+            sends.append(copy)
+
+    def wait_chip(into, send, recv):
+        for k, mate in enumerate(mates):
+            remote(into.at[mate], into.at[mate], send.at[k], recv.at[mate], chip_id(mate)).wait_recv()
+
+    send_dp(lambda peer: history, hist_buf, hist_send, hist_recv)
+    hist_buf[here] = history[...]
+
+    owner_row = owner[...]
+    pool = owner_row.shape[1]
+    div = (owner_row // item_rows).astype(f32)
+    mod = (owner_row % item_rows).astype(f32)
+    parts = jnp.where(iota((8, pool), 0) == 0, div, mod).astype(bf16)
+
+    own = stored_rows(history[...], parts, item_rows)
+    match = (iota((pool, hist_rows), 0).astype(f32) == own).astype(f32)
+    wants = [
+        jnp.max(match[e * item_rows : (e + 1) * item_rows], axis=1, keepdims=True)
+        for e in range(groups)
+    ]
+    one_hot = slots(wants, item_rows)
+    lane = iota((item_rows, 128), 1)
+    stacked = jnp.concatenate(
+        [jnp.where(lane // CAP == e, one_hot, 0.0) for e in range(groups)], axis=0
+    )
+    place = dot(stacked.astype(bf16), match.astype(bf16), 0, 0)[:rows]
+    place = place.astype(bf16)
+
+    loads[0].wait()
+    sum_buf[chip] = dot(place, grad_buf[...]).astype(bf16)
+    send_chip(lambda mate: sum_buf.at[chip], sum_buf, sum_send, sum_recv)
+
+    w_copy = remote(weight, w_buf.at[core], w_sem.at[0], w_sem.at[1], sibling)
+    w_copy.start()
+
+    loads[1].wait()
+    hidden = hidden_buf[...].astype(f32)
+    item_scale = lax.rsqrt(jnp.mean(hidden * hidden, axis=1, keepdims=True) + 1e-6)
+    item_emb = (hidden * item_scale * item_gain[...]).astype(bf16)
+
+    wait_dp(hist_buf, hist_send, hist_recv)
+    base = (here * item_rows).astype(f32)
+    local_rows = iota((item_rows, hist_rows), 0).astype(f32) + base
+    wants = []
+    for t in range(groups):
+        stored = stored_rows(hist_buf[t], parts, item_rows)
+        wants.append(jnp.max((local_rows == stored).astype(f32), axis=1, keepdims=True))
+    select = slots(wants, item_rows)[:, :rows].astype(bf16)
+    outgoing = dot(select, item_emb, 0, 0)
+    for t in range(groups):
+        emb_out[t] = fold(outgoing[t * CAP : (t + 1) * CAP]).astype(bf16)
+    send_dp(lambda peer: emb_out.at[peer], emb_in, emb_send, emb_recv)
+    emb_in[here] = emb_out[here]
+    wait_dp(emb_in, emb_send, emb_recv)
+
+    x = jnp.concatenate([unfold(emb_in[e].astype(f32)) for e in range(groups)], axis=0)
+    scale = lax.rsqrt(jnp.mean(x * x, axis=1, keepdims=True) + 1e-6)
+    normed = (x * scale * user_gain[...]).astype(bf16)
+    for p in range(chips):
+        x_out[p] = normed[:, p * piece : (p + 1) * piece]
+    send_chip(lambda mate: x_out.at[mate], x_in, x_send, x_recv)
+    x_in[chip] = x_out[chip]
+
+    loads[2].wait()
+    w_copy.wait()
+    w_all = w_buf[...].reshape(piece, -1)
+
+    wait_chip(sum_buf, sum_send, sum_recv)
+    up = dot(sum_buf[...].reshape(chips * rows, -1), w_all, 1, 1)
+    up_out[...] = up.reshape(chips, rows, piece)
+    send_chip(lambda mate: up_out.at[mate], up_in, up_send, up_recv)
+    up_in[chip] = up_out[chip]
+
+    wait_chip(x_in, x_send, x_recv)
+    part = dot(x_in[...].reshape(chips * rows, piece), w_all).reshape(chips, rows, -1)
+    part_own[...] = part
+    part_out[...] = part.astype(bf16)
+    send_chip(lambda mate: part_out.at[mate], part_in, part_send, part_recv)
+
+    wait_chip(up_in, up_send, up_recv)
+    upstream = jnp.concatenate([up_in[p] for p in range(chips)], axis=1)
+    unit = x * scale
+    scaled = upstream * user_gain[...]
+    block_sum = scale * (scaled - unit * jnp.mean(scaled * unit, axis=1, keepdims=True))
+    for t in range(groups):
+        back_out[t] = fold(block_sum[t * CAP : (t + 1) * CAP]).astype(bf16)
+    send_dp(lambda peer: back_out.at[peer], back_in, back_send, back_recv)
+    back_in[here] = back_out[here]
+
+    wait_dp(back_in, back_send, back_recv)
+    returned = jnp.concatenate([unfold(back_in[t].astype(f32)) for t in range(groups)], axis=0)
+    emb_grad = dot(select, returned.astype(bf16))
+    hidden = hidden_buf[...].astype(f32)
+    unit = hidden * item_scale
+    scaled = emb_grad * item_gain[...]
+    item_grad_out[...] = item_scale * (
+        scaled - unit * jnp.mean(scaled * unit, axis=1, keepdims=True)
+    )
+
+    wait_chip(part_in, part_send, part_recv)
+    total = part_own[chip]
+    for mate in mates:
+        total = total + part_in[mate].astype(f32)
+    values_out[...] = dot(place, total.astype(bf16), 0, 0).astype(bf16)
+
+    for copy in sends:
+        copy.wait_send()
+
+
+def local_moving_rows(
+    item_hidden, item_gain, history, owner_map, user_gain, value_weight, value_grad
+):
+    groups = lax.axis_size("dp")
+    chips = lax.axis_size("fsdp") // 2
+    item_rows, width = item_hidden.shape
+    hist_rows, out_width = value_grad.shape
+    rows = groups * CAP
+    depth = value_weight.shape[0]
+    piece = 2 * depth
+    vmem = pl.BlockSpec(memory_space=pltpu.VMEM)
+    hbm = pl.BlockSpec(memory_space=pl.ANY)
+
+    def dma(count):
+        return pltpu.SemaphoreType.DMA((count,))
+
+    return pl.pallas_call(
+        functools.partial(kernel, groups, chips),
+        out_shape=(
+            jax.ShapeDtypeStruct((hist_rows, out_width), bf16),
+            jax.ShapeDtypeStruct((item_rows, width), f32),
+        ),
+        in_specs=[vmem] * 4 + [hbm] * 3,
+        out_specs=(vmem, vmem),
+        scratch_shapes=[
+            pltpu.VMEM((item_rows, width), bf16),
+            pltpu.VMEM((hist_rows, out_width), bf16),
+            pltpu.VMEM((2, depth, out_width), bf16),
+            pltpu.VMEM((groups, 1, hist_rows), jnp.int32),
+            pltpu.VMEM((groups, 2 * CAP, width // 2), bf16),
+            pltpu.VMEM((groups, 2 * CAP, width // 2), bf16),
+            pltpu.VMEM((chips, rows, out_width), bf16),
+            pltpu.VMEM((chips, rows, piece), bf16),
+            pltpu.VMEM((chips, rows, piece), bf16),
+            pltpu.VMEM((chips, rows, out_width), f32),
+            pltpu.VMEM((chips, rows, out_width), bf16),
+            pltpu.VMEM((chips, rows, out_width), bf16),
+            pltpu.VMEM((chips, rows, piece), f32),
+            pltpu.VMEM((chips, rows, piece), f32),
+            pltpu.VMEM((groups, 2 * CAP, width // 2), bf16),
+            pltpu.VMEM((groups, 2 * CAP, width // 2), bf16),
+            dma(3), dma(2),
+            dma(groups), dma(groups), dma(groups), dma(groups),
+            dma(chips), dma(chips), dma(chips), dma(chips),
+            dma(chips), dma(chips), dma(chips), dma(chips),
+            dma(groups), dma(groups),
+        ],
+        compiler_params=pltpu.CompilerParams(
+            collective_id=0, has_side_effects=True, vmem_limit_bytes=40 * 2**20
+        ),
+    )(
+        item_gain[None, :], history[None, :], owner_map, user_gain[None, :],
+        item_hidden, value_weight, value_grad,
+    )
+
+
+def local(item_hidden, item_gain, history, owner_map, user_gain, value_weight, value_grad):
+    chips = lax.axis_size("fsdp") // 2
+    moved = 2 * chips * lax.axis_size("dp") * CAP
+    by_rows = moved <= value_grad.shape[1] and lax.axis_size("dp") * CAP <= 128
+    plan = local_moving_rows if by_rows else local_moving_weight
+    return plan(
+        item_hidden, item_gain, history, owner_map, user_gain, value_weight, value_grad
+    )
+
+
 def solution(mesh):
     in_specs = (
         P(("dp", "fsdp"), None),

time: 94.6 us -> 34.4 us (0.36)
  waiting for transfers between devices: 37.3 us -> 0 us
  Pallas kernels: 0 us -> 26.6 us
  matrix products: 15.5 us -> 0 us
  between operations: 14.1 us -> 0.66 us
  blocking collectives: 12.7 us -> 0 us
  starting transfers between devices: 8.09 us -> 0 us
  local copies, waits for them, and re-layouts: 1.12 us -> 6.86 us
  other arithmetic: 5.2 us -> 0 us
    all_gather x1 -> x0, waiting for transfers between devices: 31.5 us -> none  [local(): whole = lax.all_gather(value_weight, 'fsdp', axis=0, tiled=True)]
    pallas_call x0 -> x1, Pallas kernels: none -> 26.6 us  [local_moving_rows(): pl.pallas_call(functools.partial(kernel, groups, chips), out_shape=(jax.S...]
    dot_general x5 -> x0, matrix products: 15.5 us -> none  [the longest x1 6.36 us: local(): lax.dot_general(value_grad, whole, (((1,), (1,)), ((), ())), preferred_el...]
    all_gather x1 -> x0, blocking collectives: 12.7 us -> none  [local(): all_history = lax.all_gather(history, 'dp', axis=0, tiled=True)]
    all_to_all x2 -> x0, starting transfers between devices: 8.05 us -> none  [the longest x1 4.73 us: local(): lax.all_to_all(summed.astype(jnp.bfloat16).reshape(groups, CAP, width), '...]
    unnamed x8 -> x16, local copies, waits for them, and re-layouts: 0.02 us -> 6.86 us
    all_to_all x2 -> x0, waiting for transfers between devices: 5.1 us -> none  [the longest x1 4.25 us: local(): lax.all_to_all(outgoing, 'dp', split_axis=0, concat_axis=0, tiled=True)]
    reduce_sum x5 -> x0, other arithmetic: 3.34 us -> none  [the longest x2 1.76 us: locate(): return jnp.sum(jnp.where(matches, owner_row[None, :], 0), axis=1)]
  transfers between devices with their start and end apart: 3 -> 0, of which waited for: 3 -> 0; matrix products, arithmetic and copies ran while one was open for 13% -> 0% of each run, Pallas kernels for 0% -> 0%
where the time goes in v1:
time: 34.4 us; the launch traced here: 34.1 us
  Pallas kernels  26.6 us (77%)
  local copies, waits for them, and re-layouts  6.86 us (20%)
  between operations  0.66 us (2%)
    pallas_call x1, Pallas kernels, local_moving_rows(): pl.pallas_call(functools.partial(kernel, groups, chips), out_shape=(jax.S...  26.6 us
    unnamed x16, local copies, waits for them, and re-layouts  6.86 us

profile of v1, /device:TPU:0, one launch (start us, length us, event | category | flops | bytes accessed | tf_op | source)
XLA Modules:
  0.0 34.1 jit_solution(7206794090365343432)
XLA Ops:
  0.6 0.0 copy-start.5
  0.6 0.0 copy-start.6
  0.7 0.7 %copy-done.5 = s32[1,256]{1,0:T(1,128)S(1)} copy-done((s32[1,256]{1,0:T(1,128)S(1)}, s32[1,256]{1,0:T(1,128)}, u32[]{:S(2)}) %copy-start.5) | copy-done | bytes 1048
  1.3 0.0 copy-done.6
  1.3 0.0 copy-start
  1.3 1.2 %copy-done = bf16[256,2048]{1,0:T(8,128)(2,1)S(1)} copy-done((bf16[256,2048]{1,0:T(8,128)(2,1)S(1)}, bf16[256,2048]{1,0:T(8,128)(2,1)}, u32[]{:S(2)}) %copy-start) | copy-done | bytes 1048600
  2.5 0.0 copy-start.1
  2.5 1.0 %copy-done.1 = bf16[128,2048]{1,0:T(8,128)(2,1)S(1)} copy-done((bf16[128,2048]{1,0:T(8,128)(2,1)S(1)}, bf16[128,2048]{1,0:T(8,128)(2,1)}, u32[]{:S(2)}) %copy-start.1) | copy-done | bytes 524312
  3.6 0.0 copy-start.2
  3.6 0.9 %copy-done.2 = bf16[64,2048]{1,0:T(8,128)(2,1)S(1)} copy-done((bf16[64,2048]{1,0:T(8,128)(2,1)S(1)}, bf16[64,2048]{1,0:T(8,128)(2,1)}, u32[]{:S(2)}) %copy-start.2) | copy-done | bytes 262168
  4.5 0.0 copy-start.3
  4.5 0.7 %copy-done.3 = f32[2048]{0:T(1024)S(1)} copy-done((f32[2048]{0:T(1024)S(1)}, f32[2048]{0:T(1024)}, u32[]{:S(2)}) %copy-start.3) | copy-done | bytes 8216
  5.2 0.0 copy-start.4
  5.2 0.7 %copy-done.4 = f32[2048]{0:T(1024)S(1)} copy-done((f32[2048]{0:T(1024)S(1)}, f32[2048]{0:T(1024)}, u32[]{:S(2)}) %copy-start.4) | copy-done | bytes 8216
  5.9 26.6 %shard_map.86 = (bf16[128,2048]{1,0:T(8,128)(2,1)S(1)}, f32[64,2048]{1,0:T(8,128)S(1)}) custom-call(f32[1,2048]{1,0:T(1,128)S(1)} %bitcast.3, s32[1,128]{1,0:T(1,128)S(1)} %bitcast.5, s32[1,256]{1,0:T(1,128)S(1)} %copy-done.5, f32[1,2048]{1,0:T(1,128)S(1)} %bitcast.4, bf16[64,2048]{1,0:T(8,128)(2,1)S(1)} %copy-done.2, bf16[256,2048]{1,0:T(8,128)(2,1)S(1)} %copy-done, ...), custom_call_target="tpu_custom_call" | custom-call | tf_op jit(solution)/shard_map/pallas_call | solution.py:319
  32.5 0.8 %copy.11 = bf16[128,2048]{1,0:T(8,128)(2,1)} copy(bf16[128,2048]{1,0:T(8,128)(2,1)S(1)} %get-tuple-element.4) | data formatting | bytes 1048576
  33.3 0.8 %copy.12 = f32[64,2048]{1,0:T(8,128)} copy(f32[64,2048]{1,0:T(8,128)S(1)} %get-tuple-element.5) | data formatting | bytes 1048576
Async XLA Ops:
  0.6 0.7 %copy-start.5 = (s32[1,256]{1,0:T(1,128)S(1)}, s32[1,256]{1,0:T(1,128)}, u32[]{:S(2)}) copy-start(s32[1,256]{1,0:T(1,128)} %owner.1) | copy-start | bytes 3076
  0.6 0.7 %copy-start.6 = (s32[128]{0:T(128)S(1)}, s32[128]{0:T(128)}, u32[]{:S(2)}) copy-start(s32[128]{0:T(128)} %param.9) | copy-start | bytes 1540
  1.3 1.2 %copy-start = (bf16[256,2048]{1,0:T(8,128)(2,1)S(1)}, bf16[256,2048]{1,0:T(8,128)(2,1)}, u32[]{:S(2)}) copy-start(bf16[256,2048]{1,0:T(8,128)(2,1)} %weight.1) | copy-start | bytes 3145732
  2.5 1.0 %copy-start.1 = (bf16[128,2048]{1,0:T(8,128)(2,1)S(1)}, bf16[128,2048]{1,0:T(8,128)(2,1)}, u32[]{:S(2)}) copy-start(bf16[128,2048]{1,0:T(8,128)(2,1)} %value_grad.1) | copy-start | bytes 1572868
  3.6 0.9 %copy-start.2 = (bf16[64,2048]{1,0:T(8,128)(2,1)S(1)}, bf16[64,2048]{1,0:T(8,128)(2,1)}, u32[]{:S(2)}) copy-start(bf16[64,2048]{1,0:T(8,128)(2,1)} %item_hidden.1) | copy-start | bytes 786436
  4.5 0.7 %copy-start.3 = (f32[2048]{0:T(1024)S(1)}, f32[2048]{0:T(1024)}, u32[]{:S(2)}) copy-start(f32[2048]{0:T(1024)} %param.8) | copy-start | bytes 24580
  5.2 0.7 %copy-start.4 = (f32[2048]{0:T(1024)S(1)}, f32[2048]{0:T(1024)}, u32[]{:S(2)}) copy-start(f32[2048]{0:T(1024)} %param.11) | copy-start | bytes 24580
